TPU v7x, 32 devices: a whole 2x2x4 slice. The times are simulated.
32 devices in a mesh: groups: 2 (over x), chan: 16 (over z, y, core).
Axes of the slice: x: 2, y: 2, z: 4, core: 2. Of those that a mesh axis runs over, the one named last changes fastest.
Arguments:
- voltages: int32 [4096, 79, 2048], P(('groups', 'chan')), parts along dimension 0, may hold values from -96 to 96, as said below
- input_mask: int32 [4096], P(('groups', 'chan')), parts along dimension 0, may hold values 0 or 1
- fir_taps: float32 [16, 2048], replicated, may hold values from -1.5 to 1.5
Outputs:
- visibilities: bfloat16 [32768, 2048], P(('groups', 'chan')), parts along dimension 0
There are 2 independent parts, one for each index of `groups`. A program takes and returns all parts, laid end to end along the dimension named above; an argument that names none is the same for every part. Nothing has to cross between parts.
Inputs may be any that keep to these rules, and one draw needn't show every extreme that they name: `voltages`: 8-bit voltage samples; each input's amplitude, colour and share of a common signal differ.
All inputs are finite; a program needn't handle non-finite values. No bound on the sum of `input_mask` on one device may be relied on, other than what follows from the above.
Results may differ from a plain program's by a relative error of at most 0.006.
Values may be sent and summed in bfloat16 or wider, within the bound.
A program may use at most 320 MiB of HBM per device.

v0:
```python
from functools import reduce
import math

import jax
import jax.numpy as jnp
from jax import lax
from jax.sharding import PartitionSpec as P

INPUTS = 2048
NFFT = 2048
TAPS = 16
SPEC = 64


epsilon = 1e-05


def swapped(value, axis, stride):
    return lax.ppermute(value, axis, [(i, i ^ 1 << stride) for i in range(lax.axis_size(axis))])


def dft_matrix(length, channels):
    column = jnp.arange(length, dtype=jnp.int32)[:, None]
    channel = jnp.arange(1, channels + 1, dtype=jnp.int32)[None, :]
    phases = column * channel % length
    angles = phases.astype(jnp.float32) * (2.0 * math.pi / length)
    return jnp.concatenate([jnp.cos(angles), -jnp.sin(angles)], axis=1).astype(jnp.bfloat16)


def add_terms(left, right):
    return left + right


def polyphase(voltages, input_mask, fir_taps):
    samples = (voltages * input_mask[:, None, None]).astype(jnp.bfloat16)
    terms = [
        fir_taps[offset][None, None, :] * samples[:, offset : offset + SPEC, :]
        for offset in range(TAPS)
    ]
    filtered = reduce(add_terms, terms)
    return filtered.astype(jnp.bfloat16)


def contract(left, right):
    return lax.dot_general(
        left, right, (((1,), (1,)), ((), ())), preferred_element_type=jnp.float32
    )


def on_device(voltages, input_mask, fir_taps):
    devices = lax.axis_size("chan")
    channels = devices // 2
    local_inputs = voltages.shape[0]
    filtered = polyphase(voltages, input_mask, fir_taps)
    spectra = jnp.einsum(
        "isn,nk->iks", filtered, dft_matrix(NFFT, channels), preferred_element_type=jnp.float32
    )
    squares = jnp.sum(spectra * spectra, axis=(0, 2))
    band_partial = squares[:channels] + squares[channels:]
    band_total = lax.psum(band_partial, "chan")
    channel_gain = lax.rsqrt(band_total / (INPUTS * SPEC) + epsilon)
    equalized = (spectra * jnp.concatenate([channel_gain, channel_gain])[None, :, None]).astype(
        jnp.bfloat16
    )
    by_channel = equalized.reshape(local_inputs, 2, channels, SPEC)
    parity = lax.axis_index("chan") % 2
    half_rows = INPUTS // 2
    half_spec = SPEC // 2
    outgoing = by_channel.reshape(local_inputs, 2, channels, 2, half_spec)
    outgoing = outgoing.transpose(2, 3, 0, 1, 4).reshape(devices, local_inputs, SPEC)
    received = lax.all_to_all(outgoing, "chan", split_axis=0, concat_axis=1, tiled=True)[0]
    real_part = received[:, :half_spec]
    imag_part = received[:, half_spec:]
    rotated = jnp.concatenate([imag_part, -real_part], axis=1)
    real_vis = contract(received, received)
    imag_vis = contract(rotated, received)
    row_index = jnp.arange(INPUTS, dtype=jnp.int32)[:, None]
    column_index = jnp.arange(INPUTS, dtype=jnp.int32)[None, :]
    packed = jnp.where(column_index <= row_index, real_vis, imag_vis)
    partner_rows = lax.dynamic_slice_in_dim(packed, (1 - parity) * half_rows, half_rows, 0)
    own_rows = lax.dynamic_slice_in_dim(packed, parity * half_rows, half_rows, 0)
    summed = own_rows + swapped(partner_rows, "chan", 0)
    return (summed / SPEC).astype(jnp.bfloat16)


def solution(mesh):
    return jax.shard_map(
        on_device,
        mesh=mesh,
        in_specs=(P(("groups", "chan"), None, None), P(("groups", "chan")), P()),
        out_specs=P(("groups", "chan"), None),
        check_vma=False,
    )
```

profile of v0, /device:TPU:0, one launch (start us, length us, event | category | flops | bytes accessed | tf_op | source)
XLA Modules:
  0.0 349.4 jit_solution(1774210906190760884)
XLA Ops:
  0.0 1.9 fusion.17
  1.9 1.0 cosine_convert_fusion
  2.8 40.1 %multiply_convert_fusion = bf16[128,79,2048]{2,0,1:T(8,128)(2,1)} fusion(s32[128,79,2048]{2,0,1:T(8,128)} %param.3, s32[128]{0:T(128)} %param.4), kind=kLoop, calls=%fused_computation | loop fusion | flops 41418752 | bytes 124256768 | tf_op jit(solution)/shard_map/convert_element_type | solution.py:35
  42.9 0.0 copy-start
  43.0 0.0 copy-start.1
  43.0 200.1 %add_convert_fusion.1.clone.5 = bf16[128,64,2048]{2,0,1:T(8,128)(2,1)} fusion(bf16[128,79,2048]{2,0,1:T(8,128)(2,1)} %multiply_convert_fusion, f32[2048]{0:T(1024)S(1)} %bitcast.59, f32[2048]{0:T(1024)S(1)} %bitcast.60, f32[2048]{0:T(1024)S(1)} %bitcast.46, f32[2048]{0:T(1024)S(1)} %bitcast.47, f32[2048]{0:T(1024)S(1)} %bitcast.48, ...), kind=kLoop, calls=%fused_computation.1.clone.clone.clone.clone.2 | loop fusion | flops 805306368 | bytes 570556416 | tf_op jit(solution)/shard_map/reduce_sum | solution.py:58
  243.1 0.0 copy-done
  243.1 0.0 copy-done.1
  243.1 14.6 %multiply_reduce_fusion = (f32[16]{0:T(128)S(1)}, f32[16,128,64]{1,0,2:T(8,128)S(1)}) fusion(bf16[2048,8]{0,1:T(8,128)(2,1)S(1)} %copy-done.1, bf16[2048,8]{0,1:T(8,128)(2,1)S(1)} %copy-done, bf16[128,64,2048]{2,0,1:T(8,128)(2,1)} %add_convert_fusion.1.clone.5), kind=kOutput, calls=%fused_computation.7 | convolution fusion | flops 537264128 | bytes 34144320 | tf_op jit(solution)/shard_map/isn,nk->iks/dot_general | solution.py:55
  257.7 0.1 slice_add_fusion
  257.8 34.9 %psum.7 = f32[8]{0:T(128)S(1)} all-reduce(f32[8]{0:T(128)S(1)} %slice_add_fusion), channel_id=1, replica_groups=mesh['groups'=2,'chan'=16] {'chan'}, use_global_device_ids=true, to_apply=%region_1.2 | all-reduce | flops 8 | bytes 64 | tf_op jit(solution)/shard_map/psum | solution.py:60
  292.7 0.1 pad_maximum_fusion
  292.8 0.1 multiply_convert_fusion.2
  292.9 0.8 copy.5
  293.7 3.7 %all-to-all-start = ((bf16[16,128,64]{1,2,0:T(8,128)(2,1)}), bf16[16,128,64]{1,2,0:T(8,128)(2,1)S(1)}, u32[]{:S(2)}, u32[]{:S(2)}) async-start(bf16[16,128,64]{1,2,0:T(8,128)(2,1)} %bitcast.20), calls=%async_computation | async-start | bytes 524288 | tf_op jit(solution)/shard_map/all_to_all | solution.py:71
  297.4 9.8 %all-to-all-done = bf16[16,128,64]{1,2,0:T(8,128)(2,1)S(1)} async-done(((bf16[16,128,64]{1,2,0:T(8,128)(2,1)}), bf16[16,128,64]{1,2,0:T(8,128)(2,1)S(1)}, u32[]{:S(2)}, u32[]{:S(2)}) %all-to-all-start) | async-done | bytes 262176 | tf_op jit(solution)/shard_map/all_to_all | solution.py:71
  307.3 2.4 fusion.15
  309.7 8.6 %fusion.1 = f32[2048,2048]{1,0:T(8,128)} fusion(f32[2048,2048]{1,0:T(8,128)S(1)} %fusion.15, bf16[2048,32]{0,1:T(8,128)(2,1)S(1)} %get-tuple-element.6, bf16[2048,32]{0,1:T(8,128)(2,1)S(1)} %get-tuple-element.5, bf16[16,128,64]{1,2,0:T(8,128)(2,1)S(1)} %all-to-all-done), kind=kOutput, calls=%fused_computation.4 | convolution fusion | flops 545783808 | bytes 34078720 | tf_op jit(solution)/shard_map/dot_general | solution.py:45
  318.3 7.7 %constant_dynamic-slice_fusion = f32[1024,2048]{1,0:T(8,128)} fusion(f32[2048,2048]{1,0:T(8,128)} %fusion.1, s32[]{:T(128)S(6)} %select_n.29), kind=kLoop, calls=%fused_computation.30 | loop fusion | bytes 16777220 | tf_op jit(solution)/shard_map/dynamic_slice | solution.py:80
  326.0 0.0 collective-permute-start
  326.0 13.5 %collective-permute-done = f32[1024,2048]{1,0:T(8,128)} collective-permute-done((f32[1024,2048]{1,0:T(8,128)}, f32[1024,2048]{1,0:T(8,128)}, u32[]{:S(2)}, u32[]{:S(2)}) %collective-permute-start) | collective-permute-done | bytes 8388640 | tf_op jit(solution)/shard_map/ppermute | solution.py:19
  339.5 10.0 %multiply_convert_fusion.1 = bf16[1024,2048]{1,0:T(8,128)(2,1)} fusion(f32[1024,2048]{1,0:T(8,128)} %collective-permute-done, f32[2048,2048]{1,0:T(8,128)} %fusion.1, s32[]{:T(128)S(6)} %select_n.28), kind=kLoop, calls=%fused_computation.5 | loop fusion | flops 6291456 | bytes 20971524 | tf_op jit(solution)/shard_map/convert_element_type | solution.py:83
  (4 shorter events, 0.1 us)
Async XLA Ops:
  42.9 200.1 %copy-start = (bf16[2048,8]{0,1:T(8,128)(2,1)S(1)}, bf16[2048,8]{0,1:T(8,128)(2,1)}, u32[]{:S(2)}) copy-start(bf16[2048,8]{0,1:T(8,128)(2,1)} %get-tuple-element.23) | copy-start | bytes 98308
  43.0 200.1 %copy-start.1 = (bf16[2048,8]{0,1:T(8,128)(2,1)S(1)}, bf16[2048,8]{0,1:T(8,128)(2,1)}, u32[]{:S(2)}) copy-start(bf16[2048,8]{0,1:T(8,128)(2,1)} %get-tuple-element.24) | copy-start | bytes 98308
  293.7 13.5 %all-to-all-start = ((bf16[16,128,64]{1,2,0:T(8,128)(2,1)}), bf16[16,128,64]{1,2,0:T(8,128)(2,1)S(1)}, u32[]{:S(2)}, u32[]{:S(2)}) async-start(bf16[16,128,64]{1,2,0:T(8,128)(2,1)} %bitcast.20), calls=%async_computation | async-start | bytes 524288 | tf_op jit(solution)/shard_map/all_to_all | solution.py:71
  326.0 13.5 %collective-permute-start = (f32[1024,2048]{1,0:T(8,128)}, f32[1024,2048]{1,0:T(8,128)}, u32[]{:S(2)}, u32[]{:S(2)}) collective-permute-start(f32[1024,2048]{1,0:T(8,128)} %constant_dynamic-slice_fusion), channel_id=1, source_target_pairs={{0,1},{1,0},{2,3},{3,2},{4,5},{5,4},{6,7},{7,6},{8,9},{9,8},{10,11... | collective-permute-start | bytes 25165832 | tf_op jit(solution)/shard_map/ppermute | solution.py:19
where the time goes:
time: 350 us; the launch traced here: 349 us
  other arithmetic  251 us (72%)
  blocking collectives  34.9 us (10%)
  matrix products  25.6 us (7%)
  waiting for transfers between devices  23.3 us (7%)
  local copies, waits for them, and re-layouts  10.4 us (3%)
  starting transfers between devices  3.72 us (1%)
    reduce_sum x1, other arithmetic, on_device(): squares = jnp.sum(spectra * spectra, axis=(0, 2))  200 us
    convert_element_type x1, other arithmetic, polyphase(): samples = (voltages * input_mask[:, None, None]).astype(jnp.bfloat16)  40.1 us
    psum x1, blocking collectives, on_device(): band_total = lax.psum(band_partial, 'chan')  34.9 us
    dot_general x1, matrix products, on_device(): jnp.einsum('isn,nk->iks', filtered, dft_matrix(NFFT, channels), preferred...  14.6 us
    ppermute x1, waiting for transfers between devices, swapped(): lax.ppermute(value, axis, [(i, i ^ 1 << stride) for i in range(lax.axis_s...  13.5 us
    dot_general x2, matrix products, contract(): lax.dot_general(left, right, (((1,), (1,)), ((), ())), preferred_element_...  10.9 us
    convert_element_type x1, other arithmetic, on_device(): return (summed / SPEC).astype(jnp.bfloat16)  9.98 us
    all_to_all x1, waiting for transfers between devices, on_device(): lax.all_to_all(outgoing, 'chan', split_axis=0, concat_axis=1, tiled=True)[0]  9.81 us
  transfers between devices with their start and end apart: 2, of which 2 were waited for; matrix products, arithmetic and copies ran while one was open for 0% of the time, Pallas kernels for 0%

commit v1 on v0

v1 whole, which is shorter than its diff:
```python
import functools
import math

import jax
import jax.numpy as jnp
import numpy as np
from jax import lax
from jax.experimental import pallas as pl
from jax.experimental.pallas import tpu as pltpu
from jax.sharding import PartitionSpec as P

epsilon = 1e-05
FRAMES_PER_STEP = 4
VMEM_LIMIT = 56 * 1024 * 1024


def dft_rows(length, channels):
    column = np.arange(length)[None, :]
    channel = np.arange(1, channels + 1)[:, None]
    angles = (column * channel % length) * (2.0 * math.pi / length)
    return np.concatenate([np.cos(angles), -np.sin(angles)], axis=0)


def spectra_kernel(steps, v_ref, fir_ref, dft_ref, mask_ref, out_ref, w_ref, acc_ref):
    step = pl.program_id(0)
    per_step, inputs, length = v_ref.shape
    taps = fir_ref.shape[0]
    columns = dft_ref.shape[0]
    channels = columns // 2
    spectra = out_ref.shape[1] // 2

    @pl.when(step == 0)
    def _():
        for t in range(taps):
            w_ref[t * columns : (t + 1) * columns, :] = (
                fir_ref[t : t + 1, :] * dft_ref[...]
            ).astype(jnp.bfloat16)
        acc_ref[...] = jnp.zeros_like(acc_ref)

    samples = v_ref[...].astype(jnp.float32).astype(jnp.bfloat16)
    products = lax.dot_general(
        w_ref[...],
        samples.reshape(per_step * inputs, length),
        (((1,), (1,)), ((), ())),
        preferred_element_type=jnp.float32,
    )
    for place in range(per_step + taps - 1):
        terms = [
            products[t * columns : (t + 1) * columns, f * inputs : (f + 1) * inputs]
            for f in range(per_step)
            for t in range(taps)
            if f + taps - 1 - t == place
        ]
        acc_ref[step * per_step + place] += functools.reduce(jnp.add, terms)

    @pl.when(step == steps - 1)
    def _():
        mask = mask_ref[...].astype(jnp.float32)
        for c in range(channels):
            for part in range(2):
                column = part * channels + c
                values = acc_ref[taps - 1 : taps - 1 + spectra, column, :] * mask
                values = values.astype(jnp.bfloat16)
                rows = slice(part * spectra, (part + 1) * spectra)
                out_ref[2 * c, rows, :] = values
                out_ref[2 * c + 1, rows, :] = values


def visibility_kernel(count, rec_ref, out_ref, z_ref, rot_ref, scale_ref):
    step = pl.program_id(0)
    sources, depth, inputs = rec_ref.shape
    spectra = depth // 2
    rows = out_ref.shape[0]
    total = z_ref.shape[1]

    @pl.when(step == 0)
    def _():
        power = jnp.zeros((depth, inputs), jnp.float32)
        for source in range(sources):
            block = rec_ref[source]
            columns = slice(source * inputs, (source + 1) * inputs)
            z_ref[:, columns] = block
            rot_ref[:spectra, columns] = -block[spectra:]
            rot_ref[spectra:, columns] = block[:spectra]
            wide = block.astype(jnp.float32)
            power = power + wide * wide
        power = jnp.sum(jnp.sum(power, axis=0, keepdims=True), axis=1, keepdims=True)
        scale = 1.0 / ((power / count + epsilon) * spectra)
        scale_ref[...] = jnp.broadcast_to(scale, scale_ref.shape)

    parity = lax.axis_index("chan") % 2
    first = pl.multiple_of(parity * (total // 2) + step * rows, rows)
    left = z_ref[:, pl.ds(first, rows)].T
    scale = scale_ref[0:1, 0:1]
    width = 512
    for start in range(0, total, width):
        columns = slice(start, start + width)
        real = jnp.dot(left, z_ref[:, columns], preferred_element_type=jnp.float32)
        imag = jnp.dot(left, rot_ref[:, columns], preferred_element_type=jnp.float32)
        row = lax.broadcasted_iota(jnp.int32, real.shape, 0) + first
        column = lax.broadcasted_iota(jnp.int32, real.shape, 1) + start
        packed = jnp.where(column <= row, real, imag)
        out_ref[:, columns] = (packed * scale).astype(jnp.bfloat16)


def on_device(voltages, input_mask, fir_taps):
    devices = lax.axis_size("chan")
    channels = devices // 2
    inputs, frames, length = voltages.shape
    taps = fir_taps.shape[0]
    spectra = frames - taps + 1
    total = inputs * devices
    steps = pl.cdiv(frames, FRAMES_PER_STEP)
    by_frame = voltages.transpose(1, 0, 2)
    dft = jnp.asarray(dft_rows(length, channels), jnp.bfloat16).astype(jnp.float32)
    outgoing = pl.pallas_call(
        functools.partial(spectra_kernel, steps),
        out_shape=jax.ShapeDtypeStruct((devices, 2 * spectra, inputs), jnp.bfloat16),
        grid=(steps,),
        in_specs=[
            pl.BlockSpec((FRAMES_PER_STEP, inputs, length), lambda i: (i, 0, 0)),
            pl.BlockSpec((taps, length), lambda i: (0, 0)),
            pl.BlockSpec((2 * channels, length), lambda i: (0, 0)),
            pl.BlockSpec((1, inputs), lambda i: (0, 0)),
        ],
        out_specs=pl.BlockSpec((devices, 2 * spectra, inputs), lambda i: (0, 0, 0)),
        scratch_shapes=[
            pltpu.VMEM((taps * 2 * channels, length), jnp.bfloat16),
            pltpu.VMEM((steps * FRAMES_PER_STEP + taps - 1, 2 * channels, inputs), jnp.float32),
        ],
        compiler_params=pltpu.CompilerParams(vmem_limit_bytes=VMEM_LIMIT),
    )(by_frame, fir_taps, dft, input_mask[None, :])
    received = lax.all_to_all(outgoing, "chan", split_axis=0, concat_axis=0, tiled=True)
    rows = 128
    return pl.pallas_call(
        functools.partial(visibility_kernel, float(total * spectra)),
        out_shape=jax.ShapeDtypeStruct((total // 2, total), jnp.bfloat16),
        grid=(total // 2 // rows,),
        in_specs=[pl.BlockSpec((devices, 2 * spectra, inputs), lambda i: (0, 0, 0))],
        out_specs=pl.BlockSpec((rows, total), lambda i: (i, 0)),
        scratch_shapes=[
            pltpu.VMEM((2 * spectra, total), jnp.bfloat16),
            pltpu.VMEM((2 * spectra, total), jnp.bfloat16),
            pltpu.VMEM((8, 128), jnp.float32),
        ],
        compiler_params=pltpu.CompilerParams(vmem_limit_bytes=VMEM_LIMIT),
    )(received)


def solution(mesh):
    return jax.shard_map(
        on_device,
        mesh=mesh,
        in_specs=(P(("groups", "chan"), None, None), P(("groups", "chan")), P()),
        out_specs=P(("groups", "chan"), None),
        check_vma=False,
    )
```

time: 350 us -> 63.3 us (0.18)
  other arithmetic: 251 us -> 0 us
  Pallas kernels: 0 us -> 40.8 us
  matrix products: 25.6 us -> 0 us
  waiting for transfers between devices: 23.3 us -> 0 us
  blocking collectives: 34.9 us -> 22 us
  local copies, waits for them, and re-layouts: 10.4 us -> 0 us
  starting transfers between devices: 3.72 us -> 0 us
    reduce_sum x1 -> x0, other arithmetic: 200 us -> none  [on_device(): squares = jnp.sum(spectra * spectra, axis=(0, 2))]
    convert_element_type x3 -> x0, other arithmetic: 50.2 us -> none  [the longest x1 40.1 us: polyphase(): samples = (voltages * input_mask[:, None, None]).astype(jnp.bfloat16)]
    pallas_call x0 -> x2, Pallas kernels: none -> 40.8 us  [the longest x1 33.7 us: on_device(): pl.pallas_call(functools.partial(spectra_kernel, steps), out_shape=jax.Sh...]
    psum x1 -> x0, blocking collectives: 34.9 us -> none  [on_device(): band_total = lax.psum(band_partial, 'chan')]
    dot_general x3 -> x0, matrix products: 25.6 us -> none  [the longest x1 14.6 us: on_device(): jnp.einsum('isn,nk->iks', filtered, dft_matrix(NFFT, channels), preferred...]
    all_to_all x0 -> x1, blocking collectives: none -> 22 us  [on_device(): lax.all_to_all(outgoing, 'chan', split_axis=0, concat_axis=0, tiled=True)]
    ppermute x1 -> x0, waiting for transfers between devices: 13.5 us -> none  [swapped(): lax.ppermute(value, axis, [(i, i ^ 1 << stride) for i in range(lax.axis_s...]
    all_to_all x1 -> x0, waiting for transfers between devices: 9.81 us -> none  [on_device(): lax.all_to_all(outgoing, 'chan', split_axis=0, concat_axis=1, tiled=True)[0]]
  transfers between devices with their start and end apart: 2 -> 0, of which waited for: 2 -> 0; matrix products, arithmetic and copies ran while one was open for 0% -> 0% of each run, Pallas kernels for 0% -> 0%
where the time goes in v1:
time: 63.3 us; the launch traced here: 62.7 us
  Pallas kernels  40.8 us (64%)
  blocking collectives  22 us (35%)
    pallas_call x1, Pallas kernels, on_device(): pl.pallas_call(functools.partial(spectra_kernel, steps), out_shape=jax.Sh...  33.7 us
    all_to_all x1, blocking collectives, on_device(): lax.all_to_all(outgoing, 'chan', split_axis=0, concat_axis=0, tiled=True)  22 us
    pallas_call x1, Pallas kernels, on_device(): pl.pallas_call(functools.partial(visibility_kernel, float(total * spectra...  7.05 us

profile of v1, /device:TPU:0, one launch (start us, length us, event | category | flops | bytes accessed | tf_op | source)
XLA Modules:
  0.0 62.7 jit_solution(11097059381267032816)
XLA Ops:
  0.0 33.7 %shard_map.46 = bf16[16,128,128]{2,1,0:T(8,128)(2,1)} custom-call(s32[79,128,2048]{2,1,0:T(8,128)} %bitcast.v_ref, f32[16,2048]{1,0:T(8,128)} %fir_ref.1, f32[16,2048]{1,0:T(8,128)} %constant.3.dft_ref, s32[1,128]{1,0:T(1,128)} %bitcast.2), custom_call_target="tpu_custom_call" | custom-call | tf_op jit(solution)/shard_map/pallas_call | solution.py:116
  33.7 22.0 %all_to_all.5.rec_ref = bf16[16,128,128]{2,1,0:T(8,128)(2,1)} all-to-all(bf16[16,128,128]{2,1,0:T(8,128)(2,1)} %shard_map.46), channel_id=1, replica_groups=mesh['groups'=2,'chan'=16] {'chan'}, dimensions={0} | all-to-all | bytes 1048576 | tf_op jit(solution)/shard_map/all_to_all | solution.py:133
  55.7 7.1 %shard_map.47 = bf16[1024,2048]{1,0:T(8,128)(2,1)} custom-call(bf16[16,128,128]{2,1,0:T(8,128)(2,1)} %all_to_all.5.rec_ref), custom_call_target="tpu_custom_call" | custom-call | tf_op jit(solution)/shard_map/pallas_call | solution.py:135

commit v2 on v1

--- a/solution.py
+++ b/solution.py
@@ -10,7 +10,7 @@
 from jax.sharding import PartitionSpec as P
 
 epsilon = 1e-05
-FRAMES_PER_STEP = 4
+FRAMES_PER_STEP = 8
 VMEM_LIMIT = 56 * 1024 * 1024
 
 
@@ -21,16 +21,32 @@
     return np.concatenate([np.cos(angles), -np.sin(angles)], axis=0)
 
 
-def spectra_kernel(steps, v_ref, fir_ref, dft_ref, mask_ref, out_ref, w_ref, acc_ref):
+def spectra_kernel(
+    steps, v_ref, fir_ref, dft_ref, mask_ref, out_ref,
+    w_ref, acc_ref, stage_ref, send_sem, recv_sem, local_sem,
+):
     step = pl.program_id(0)
     per_step, inputs, length = v_ref.shape
     taps = fir_ref.shape[0]
     columns = dft_ref.shape[0]
     channels = columns // 2
-    spectra = out_ref.shape[1] // 2
+    barrier = pltpu.get_barrier_semaphore()
 
     @pl.when(step == 0)
     def _():
+        here = lax.axis_index("chan")
+        count = lax.axis_size("chan")
+
+        def greet(offset, carry):
+            pl.semaphore_signal(
+                barrier,
+                inc=1,
+                device_id={"chan": lax.rem(here + offset, count)},
+                device_id_type=pl.DeviceIdType.MESH,
+            )
+            return carry
+
+        lax.fori_loop(1, count, greet, 0)
         for t in range(taps):
             w_ref[t * columns : (t + 1) * columns, :] = (
                 fir_ref[t : t + 1, :] * dft_ref[...]
@@ -53,22 +69,53 @@
         ]
         acc_ref[step * per_step + place] += functools.reduce(jnp.add, terms)
 
-    @pl.when(step == steps - 1)
+    devices, pieces, depth, _ = out_ref.shape
+    me = lax.axis_index("chan")
+    piece = step - (per_step + taps - 2) // per_step
+
+    @pl.when(piece == 0)
+    def _():
+        pl.semaphore_wait(barrier, devices - 1)
+
+    @pl.when(piece >= 0)
     def _():
         mask = mask_ref[...].astype(jnp.float32)
         for c in range(channels):
-            for part in range(2):
-                column = part * channels + c
-                values = acc_ref[taps - 1 : taps - 1 + spectra, column, :] * mask
-                values = values.astype(jnp.bfloat16)
-                rows = slice(part * spectra, (part + 1) * spectra)
-                out_ref[2 * c, rows, :] = values
-                out_ref[2 * c + 1, rows, :] = values
+            parts = [
+                acc_ref[pl.ds(taps - 1 + piece * per_step, per_step), column, :]
+                for column in (c, channels + c)
+            ]
+            stage_ref[c, piece] = (jnp.concatenate(parts, axis=0) * mask).astype(jnp.bfloat16)
+
+        def send(offset, carry):
+            target = lax.rem(me + offset, devices)
+            pltpu.make_async_remote_copy(
+                src_ref=stage_ref.at[target // 2, piece],
+                dst_ref=out_ref.at[me, piece],
+                send_sem=send_sem,
+                recv_sem=recv_sem,
+                device_id={"chan": target},
+                device_id_type=pl.DeviceIdType.MESH,
+            ).start()
+            return carry
+
+        lax.fori_loop(1, devices, send, 0)
+        pltpu.make_async_copy(stage_ref.at[me // 2, piece], out_ref.at[me, piece], local_sem).start()
+
+    @pl.when(step == steps - 1)
+    def _():
+        own = out_ref.at[0]
+        others = out_ref.at[pl.ds(0, devices - 1)]
+        pltpu.make_async_copy(own, own, local_sem).wait()
+        pltpu.make_async_copy(others, others, send_sem).wait()
+        pltpu.make_async_copy(others, others, recv_sem).wait()
 
 
 def visibility_kernel(count, rec_ref, out_ref, z_ref, rot_ref, scale_ref):
     step = pl.program_id(0)
-    sources, depth, inputs = rec_ref.shape
+    sources, pieces, piece_depth, inputs = rec_ref.shape
+    depth = pieces * piece_depth
+    half = piece_depth // 2
     spectra = depth // 2
     rows = out_ref.shape[0]
     total = z_ref.shape[1]
@@ -78,11 +125,12 @@
         power = jnp.zeros((depth, inputs), jnp.float32)
         for source in range(sources):
             block = rec_ref[source]
+            wide = block.astype(jnp.float32)
+            turned = jnp.concatenate([-wide[:, half:], wide[:, :half]], axis=1)
+            wide = wide.reshape(depth, inputs)
             columns = slice(source * inputs, (source + 1) * inputs)
-            z_ref[:, columns] = block
-            rot_ref[:spectra, columns] = -block[spectra:]
-            rot_ref[spectra:, columns] = block[:spectra]
-            wide = block.astype(jnp.float32)
+            z_ref[:, columns] = block.reshape(depth, inputs)
+            rot_ref[:, columns] = turned.reshape(depth, inputs).astype(jnp.bfloat16)
             power = power + wide * wide
         power = jnp.sum(jnp.sum(power, axis=0, keepdims=True), axis=1, keepdims=True)
         scale = 1.0 / ((power / count + epsilon) * spectra)
@@ -113,30 +161,38 @@
     steps = pl.cdiv(frames, FRAMES_PER_STEP)
     by_frame = voltages.transpose(1, 0, 2)
     dft = jnp.asarray(dft_rows(length, channels), jnp.bfloat16).astype(jnp.float32)
-    outgoing = pl.pallas_call(
+    pieces = spectra // FRAMES_PER_STEP
+    depth = 2 * FRAMES_PER_STEP
+    columns = 2 * channels
+    received = pl.pallas_call(
         functools.partial(spectra_kernel, steps),
-        out_shape=jax.ShapeDtypeStruct((devices, 2 * spectra, inputs), jnp.bfloat16),
+        out_shape=jax.ShapeDtypeStruct((devices, pieces, depth, inputs), jnp.bfloat16),
         grid=(steps,),
         in_specs=[
             pl.BlockSpec((FRAMES_PER_STEP, inputs, length), lambda i: (i, 0, 0)),
             pl.BlockSpec((taps, length), lambda i: (0, 0)),
-            pl.BlockSpec((2 * channels, length), lambda i: (0, 0)),
+            pl.BlockSpec((columns, length), lambda i: (0, 0)),
             pl.BlockSpec((1, inputs), lambda i: (0, 0)),
         ],
-        out_specs=pl.BlockSpec((devices, 2 * spectra, inputs), lambda i: (0, 0, 0)),
+        out_specs=pl.BlockSpec(memory_space=pl.ANY),
         scratch_shapes=[
-            pltpu.VMEM((taps * 2 * channels, length), jnp.bfloat16),
-            pltpu.VMEM((steps * FRAMES_PER_STEP + taps - 1, 2 * channels, inputs), jnp.float32),
+            pltpu.VMEM((taps * columns, length), jnp.bfloat16),
+            pltpu.VMEM((steps * FRAMES_PER_STEP + taps - 1, columns, inputs), jnp.float32),
+            pltpu.VMEM((channels, pieces, depth, inputs), jnp.bfloat16),
+            pltpu.SemaphoreType.DMA,
+            pltpu.SemaphoreType.DMA,
+            pltpu.SemaphoreType.DMA,
         ],
-        compiler_params=pltpu.CompilerParams(vmem_limit_bytes=VMEM_LIMIT),
+        compiler_params=pltpu.CompilerParams(
+            vmem_limit_bytes=VMEM_LIMIT, collective_id=0, has_side_effects=True
+        ),
     )(by_frame, fir_taps, dft, input_mask[None, :])
-    received = lax.all_to_all(outgoing, "chan", split_axis=0, concat_axis=0, tiled=True)
     rows = 128
     return pl.pallas_call(
         functools.partial(visibility_kernel, float(total * spectra)),
         out_shape=jax.ShapeDtypeStruct((total // 2, total), jnp.bfloat16),
         grid=(total // 2 // rows,),
-        in_specs=[pl.BlockSpec((devices, 2 * spectra, inputs), lambda i: (0, 0, 0))],
+        in_specs=[pl.BlockSpec((devices, pieces, depth, inputs), lambda i: (0, 0, 0, 0))],
         out_specs=pl.BlockSpec((rows, total), lambda i: (i, 0)),
         scratch_shapes=[
             pltpu.VMEM((2 * spectra, total), jnp.bfloat16),

time: 63.3 us -> 43.1 us (0.68)
  blocking collectives: 22 us -> 0 us
  Pallas kernels: 40.8 us -> 42.7 us
    all_to_all x1 -> x0, blocking collectives: 22 us -> none  [on_device(): lax.all_to_all(outgoing, 'chan', split_axis=0, concat_axis=0, tiled=True)]
    pallas_call x1, Pallas kernels: 33.7 us -> 35.6 us  [on_device(): pl.pallas_call(functools.partial(spectra_kernel, steps), out_shape=jax.Sh...]
where the time goes in v2:
time: 43.1 us; the launch traced here: 42.7 us
  Pallas kernels  42.7 us (99%)
    pallas_call x1, Pallas kernels, on_device(): pl.pallas_call(functools.partial(spectra_kernel, steps), out_shape=jax.Sh...  35.6 us
    pallas_call x1, Pallas kernels, on_device(): pl.pallas_call(functools.partial(visibility_kernel, float(total * spectra...  7.08 us

profile of v2, /device:TPU:0, one launch (start us, length us, event | category | flops | bytes accessed | tf_op | source)
XLA Modules:
  0.0 42.7 jit_solution(487138160709970227)
XLA Ops:
  0.0 35.6 %shard_map.46.rec_ref = bf16[16,8,16,128]{3,2,1,0:T(8,128)(2,1)} custom-call(s32[79,128,2048]{2,1,0:T(8,128)} %bitcast.v_ref, f32[16,2048]{1,0:T(8,128)} %fir_ref.1, f32[16,2048]{1,0:T(8,128)} %constant.3.dft_ref, s32[1,128]{1,0:T(1,128)} %bitcast.2), custom_call_target="tpu_custom_call" | custom-call | tf_op jit(solution)/shard_map/pallas_call | solution.py:167
  35.7 7.1 %shard_map.47 = bf16[1024,2048]{1,0:T(8,128)(2,1)} custom-call(bf16[16,8,16,128]{3,2,1,0:T(8,128)(2,1)} %shard_map.46.rec_ref), custom_call_target="tpu_custom_call" | custom-call | tf_op jit(solution)/shard_map/pallas_call | solution.py:191

commit v3 on v2

--- a/solution.py
+++ b/solution.py
@@ -11,6 +11,8 @@
 
 epsilon = 1e-05
 FRAMES_PER_STEP = 8
+ROWS = 512
+WIDTH = 512
 VMEM_LIMIT = 56 * 1024 * 1024
 
 
@@ -111,7 +113,7 @@
         pltpu.make_async_copy(others, others, recv_sem).wait()
 
 
-def visibility_kernel(count, rec_ref, out_ref, z_ref, rot_ref, scale_ref):
+def visibility_kernel(count, rec_ref, out_ref, z_ref, mix_ref, scale_ref):
     step = pl.program_id(0)
     sources, pieces, piece_depth, inputs = rec_ref.shape
     depth = pieces * piece_depth
@@ -119,6 +121,7 @@
     spectra = depth // 2
     rows = out_ref.shape[0]
     total = z_ref.shape[1]
+    start_row = (lax.axis_index("chan") % 2) * (total // 2)
 
     @pl.when(step == 0)
     def _():
@@ -127,28 +130,30 @@
             block = rec_ref[source]
             wide = block.astype(jnp.float32)
             turned = jnp.concatenate([-wide[:, half:], wide[:, :half]], axis=1)
+            mixed = jnp.where(source * inputs < start_row, wide, turned)
             wide = wide.reshape(depth, inputs)
             columns = slice(source * inputs, (source + 1) * inputs)
             z_ref[:, columns] = block.reshape(depth, inputs)
-            rot_ref[:, columns] = turned.reshape(depth, inputs).astype(jnp.bfloat16)
+            mix_ref[:, columns] = mixed.reshape(depth, inputs).astype(jnp.bfloat16)
             power = power + wide * wide
         power = jnp.sum(jnp.sum(power, axis=0, keepdims=True), axis=1, keepdims=True)
         scale = 1.0 / ((power / count + epsilon) * spectra)
         scale_ref[...] = jnp.broadcast_to(scale, scale_ref.shape)
 
-    parity = lax.axis_index("chan") % 2
-    first = pl.multiple_of(parity * (total // 2) + step * rows, rows)
-    left = z_ref[:, pl.ds(first, rows)].T
+    diagonal = pl.ds(pl.multiple_of(start_row + step * rows, rows), rows)
+    own = z_ref[:, diagonal]
+    left = own.T
     scale = scale_ref[0:1, 0:1]
-    width = 512
-    for start in range(0, total, width):
-        columns = slice(start, start + width)
-        real = jnp.dot(left, z_ref[:, columns], preferred_element_type=jnp.float32)
-        imag = jnp.dot(left, rot_ref[:, columns], preferred_element_type=jnp.float32)
-        row = lax.broadcasted_iota(jnp.int32, real.shape, 0) + first
-        column = lax.broadcasted_iota(jnp.int32, real.shape, 1) + start
-        packed = jnp.where(column <= row, real, imag)
-        out_ref[:, columns] = (packed * scale).astype(jnp.bfloat16)
+    for start in range(0, total, WIDTH):
+        columns = slice(start, start + WIDTH)
+        values = jnp.dot(left, mix_ref[:, columns], preferred_element_type=jnp.float32)
+        out_ref[:, columns] = (values * scale).astype(jnp.bfloat16)
+    real = jnp.dot(left, own, preferred_element_type=jnp.float32) * scale
+    row = lax.broadcasted_iota(jnp.int32, real.shape, 0)
+    column = lax.broadcasted_iota(jnp.int32, real.shape, 1)
+    imag = out_ref[:, diagonal].astype(jnp.float32)
+    out_ref[:, diagonal] = jnp.where(column <= row, real, imag).astype(jnp.bfloat16)
+    mix_ref[:, diagonal] = own
 
 
 def on_device(voltages, input_mask, fir_taps):
@@ -187,13 +192,12 @@
             vmem_limit_bytes=VMEM_LIMIT, collective_id=0, has_side_effects=True
         ),
     )(by_frame, fir_taps, dft, input_mask[None, :])
-    rows = 128
     return pl.pallas_call(
         functools.partial(visibility_kernel, float(total * spectra)),
         out_shape=jax.ShapeDtypeStruct((total // 2, total), jnp.bfloat16),
-        grid=(total // 2 // rows,),
+        grid=(total // 2 // ROWS,),
         in_specs=[pl.BlockSpec((devices, pieces, depth, inputs), lambda i: (0, 0, 0, 0))],
-        out_specs=pl.BlockSpec((rows, total), lambda i: (i, 0)),
+        out_specs=pl.BlockSpec((ROWS, total), lambda i: (i, 0)),
         scratch_shapes=[
             pltpu.VMEM((2 * spectra, total), jnp.bfloat16),
             pltpu.VMEM((2 * spectra, total), jnp.bfloat16),

time: 43.1 us -> 40.6 us (0.942)
  Pallas kernels: 42.7 us -> 40.2 us
    pallas_call x1, Pallas kernels: 7.08 us -> 4.59 us  [on_device(): pl.pallas_call(functools.partial(visibility_kernel, float(total * spectra...]
where the time goes in v3:
time: 40.6 us; the launch traced here: 40.2 us
  Pallas kernels  40.2 us (99%)
    pallas_call x1, Pallas kernels, on_device(): pl.pallas_call(functools.partial(spectra_kernel, steps), out_shape=jax.Sh...  35.6 us
    pallas_call x1, Pallas kernels, on_device(): pl.pallas_call(functools.partial(visibility_kernel, float(total * spectra...  4.59 us

profile of v3, /device:TPU:0, one launch (start us, length us, event | category | flops | bytes accessed | tf_op | source)
XLA Modules:
  0.0 40.2 jit_solution(6362253203782048649)
XLA Ops:
  0.0 35.6 %shard_map.46.rec_ref = bf16[16,8,16,128]{3,2,1,0:T(8,128)(2,1)} custom-call(s32[79,128,2048]{2,1,0:T(8,128)} %bitcast.v_ref, f32[16,2048]{1,0:T(8,128)} %fir_ref.1, f32[16,2048]{1,0:T(8,128)} %constant.3.dft_ref, s32[1,128]{1,0:T(1,128)} %bitcast.2), custom_call_target="tpu_custom_call" | custom-call | tf_op jit(solution)/shard_map/pallas_call | solution.py:172
  35.7 4.6 %shard_map.47 = bf16[1024,2048]{1,0:T(8,128)(2,1)} custom-call(bf16[16,8,16,128]{3,2,1,0:T(8,128)(2,1)} %shard_map.46.rec_ref), custom_call_target="tpu_custom_call" | custom-call | tf_op jit(solution)/shard_map/pallas_call | solution.py:195

commit v4 on v3

--- a/solution.py
+++ b/solution.py
@@ -13,7 +13,7 @@
 FRAMES_PER_STEP = 8
 ROWS = 512
 WIDTH = 512
-VMEM_LIMIT = 56 * 1024 * 1024
+VMEM_LIMIT = 28 * 1024 * 1024
 
 
 def dft_rows(length, channels):

time: 40.6 us -> 41.7 us (1.027)
  local copies, waits for them, and re-layouts: 0 us -> 2.46 us
  Pallas kernels: 40.2 us -> 39 us
    unnamed x0 -> x6, local copies, waits for them, and re-layouts: none -> 2.46 us
    pallas_call x1, Pallas kernels: 4.59 us -> 3.56 us  [on_device(): pl.pallas_call(functools.partial(visibility_kernel, float(total * spectra...]
where the time goes in v4:
time: 41.7 us; the launch traced here: 41.5 us
  Pallas kernels  39 us (94%)
  local copies, waits for them, and re-layouts  2.46 us (6%)
    pallas_call x1, Pallas kernels, on_device(): pl.pallas_call(functools.partial(spectra_kernel, steps), out_shape=jax.Sh...  35.4 us
    pallas_call x1, Pallas kernels, on_device(): pl.pallas_call(functools.partial(visibility_kernel, float(total * spectra...  3.56 us
    unnamed x6, local copies, waits for them, and re-layouts  2.46 us

profile of v4, /device:TPU:0, one launch (start us, length us, event | category | flops | bytes accessed | tf_op | source)
XLA Modules:
  0.0 41.5 jit_solution(8322530807967028638)
XLA Ops:
  0.0 0.0 copy-start
  0.0 0.9 %copy-done = f32[16,2048]{1,0:T(8,128)S(1)} copy-done((f32[16,2048]{1,0:T(8,128)S(1)}, f32[16,2048]{1,0:T(8,128)}, u32[]{:S(2)}) %copy-start) | copy-done | bytes 131096
  0.9 0.0 copy-start.1
  0.9 0.9 %copy-done.1 = f32[16,2048]{1,0:T(8,128)S(1)} copy-done((f32[16,2048]{1,0:T(8,128)S(1)}, f32[16,2048]{1,0:T(8,128)}, u32[]{:S(2)}) %copy-start.1) | copy-done | bytes 131096
  1.8 0.0 copy-start.2
  1.8 0.7 %copy-done.2 = s32[128]{0:T(128)S(1)} copy-done((s32[128]{0:T(128)S(1)}, s32[128]{0:T(128)}, u32[]{:S(2)}) %copy-start.2) | copy-done | bytes 536
  2.5 35.4 %shard_map.46.rec_ref = bf16[16,8,16,128]{3,2,1,0:T(8,128)(2,1)S(1)} custom-call(s32[79,128,2048]{2,1,0:T(8,128)} %bitcast.v_ref, f32[16,2048]{1,0:T(8,128)S(1)} %copy-done, f32[16,2048]{1,0:T(8,128)S(1)} %copy-done.1, s32[1,128]{1,0:T(1,128)S(1)} %bitcast.2), custom_call_target="tpu_custom_call" | custom-call | tf_op jit(solution)/shard_map/pallas_call | solution.py:172
  37.9 3.6 %shard_map.47 = bf16[1024,2048]{1,0:T(8,128)(2,1)} custom-call(bf16[16,8,16,128]{3,2,1,0:T(8,128)(2,1)S(1)} %shard_map.46.rec_ref), custom_call_target="tpu_custom_call" | custom-call | tf_op jit(solution)/shard_map/pallas_call | solution.py:195
Async XLA Ops:
  0.0 0.9 %copy-start = (f32[16,2048]{1,0:T(8,128)S(1)}, f32[16,2048]{1,0:T(8,128)}, u32[]{:S(2)}) copy-start(f32[16,2048]{1,0:T(8,128)} %fir_ref.1) | copy-start | bytes 393220
  0.9 0.9 %copy-start.1 = (f32[16,2048]{1,0:T(8,128)S(1)}, f32[16,2048]{1,0:T(8,128)}, u32[]{:S(2)}) copy-start(f32[16,2048]{1,0:T(8,128)} %constant.3.dft_ref) | copy-start | bytes 393220
  1.8 0.7 %copy-start.2 = (s32[128]{0:T(128)S(1)}, s32[128]{0:T(128)}, u32[]{:S(2)}) copy-start(s32[128]{0:T(128)} %param.5) | copy-start | bytes 1540
